TPU v7x, 32 devices: a whole 2x2x4 slice. The times are simulated.
32 devices in a mesh: seg: 4 (over y, x), block: 8 (over z, core).
Axes of the slice: x: 2, y: 2, z: 4, core: 2. Of those that a mesh axis runs over, the one named last changes fastest.
Arguments:
- jacobian: float32 [128, 128, 128], P(('seg', 'block')), may hold values from -2 to 2
- implicit_inv: float32 [128, 128, 128], P(('seg', 'block')), may hold values from -2 to 2, as said below
- input_map: float32 [128, 128, 64], P(('seg', 'block')), may hold values from -0.75 to 0.75
- controls: float32 [128, 64], P(('seg', 'block')), may hold values from -2 to 2
- control_step: float32 [128, 64], P(('seg', 'block')), may hold values from -2 to 2
- state_traj: float32 [128, 128], P(('seg', 'block')), may hold values from -2 to 2
- terminal: float32 [128], replicated, may hold values from -2 to 2
- init_gap: float32 [128], replicated, may hold values from -3 to 3
- counts: int32 [32], P(('seg', 'block')), may hold values from 2 to 4, as said below
Outputs:
- updated: float32 [128, 128], P(('seg', 'block'))
- defect_out: float32 [128, 128], P(('seg', 'block'))
Inputs may be any that keep to these rules, and one draw needn't show every extreme that they name: implicit_inv[k] is the inverse of I - jacobian[k] / 2 + jacobian[k] jacobian[k] / 12. `counts`: some block uses all 4 slots and some only half of 4, rounded down; used slots are the first ones of a block.
All inputs are finite; a program needn't handle non-finite values.
Results may differ from a plain program's by a relative error of at most 0.0003.
Values sent between devices are 32-bit elements; how exact they have to be, the bound alone decides.
A program may use at most 64 MiB of HBM per device.

v0:
```python
import jax
import jax.numpy as jnp
from jax import lax
from jax.sharding import PartitionSpec as P

highest = lax.Precision.HIGHEST


def from_behind(value, axis, by):
    size = lax.axis_size(axis)
    pairs = [(i, i + by) for i in range(size) if 0 <= i + by < size]
    return lax.ppermute(value, axis, pairs)


def entering(part, axis, combine, identity):
    place = lax.axis_index(axis)
    gathered = jax.tree.map(lambda a: lax.all_gather(a, axis), part)
    state = jax.tree.map(lambda a, e: jnp.zeros_like(a) + jnp.asarray(e, a.dtype), part, identity)

    def one(lap, state):
        return combine(
            state, jax.tree.map(lambda a: lax.dynamic_index_in_dim(a, lap, 0, False), gathered)
        )

    return lax.fori_loop(0, place, one, state)


def spread(value, axis, source):
    kept = jnp.where(lax.axis_index(axis) == source, value, 0).astype(value.dtype)
    return lax.psum(kept, axis)


def batch_matrix(left, right):
    return jnp.einsum("kij,kjl->kil", left, right, precision=highest)


def batch_vector(matrices, vectors):
    return jnp.einsum("kij,kj->ki", matrices, vectors, precision=highest)


def compose(earlier, later):
    return (
        jnp.dot(later[0], earlier[0], precision=highest),
        jnp.dot(later[0], earlier[1], precision=highest) + later[1],
    )


def tree_fold(matrices, vectors):
    while matrices.shape[0] > 1:
        earlier_m = matrices[0::2]
        later_m = matrices[1::2]
        earlier_v = vectors[0::2]
        later_v = vectors[1::2]
        matrices = batch_matrix(later_m, earlier_m)
        vectors = batch_vector(later_m, earlier_v) + later_v
    return (matrices[0], vectors[0])


def body(
    jacobian,
    implicit_inv,
    input_map,
    controls,
    control_step,
    state_traj,
    terminal,
    init_gap,
    counts,
):
    knot_count, state_width = state_traj.shape
    devices = lax.axis_size(("seg", "block"))
    position = lax.axis_index(("seg", "block"))
    upcoming = from_behind(state_traj[0], ("seg", "block"), -1)
    upcoming = jnp.where(position == devices - 1, terminal, upcoming)
    slot_ids = jnp.arange(knot_count)
    active = slot_ids < counts[0]
    following = jnp.concatenate([state_traj[1:], upcoming[None]], axis=0)
    next_state = jnp.where((slot_ids + 1 < counts[0])[:, None], following, upcoming[None])
    squared = batch_matrix(jacobian, jacobian)
    identity = jnp.eye(state_width, dtype=jnp.float32)
    explicit = identity + 0.5 * jacobian + squared / 12.0
    implicit_x = (
        next_state
        - 0.5 * batch_vector(jacobian, next_state)
        + batch_vector(squared, next_state) / 12.0
    )
    defect = implicit_x - batch_vector(explicit, state_traj) - batch_vector(input_map, controls)
    transition = batch_matrix(implicit_inv, explicit)
    offset = batch_vector(implicit_inv, batch_vector(input_map, control_step) - defect)
    transition = jnp.where(active[:, None, None], transition, identity[None])
    offset = jnp.where(active[:, None], offset, 0.0)
    neutral = (identity, jnp.zeros((state_width,), jnp.float32))
    element = tree_fold(transition, offset)
    within = entering(element, "block", compose, neutral)
    through = compose(within, element)
    segment_total = (
        spread(through[0], "block", lax.axis_size("block") - 1),
        spread(through[1], "block", lax.axis_size("block") - 1),
    )
    before = entering(segment_total, "seg", compose, neutral)
    prefix = compose(before, within)
    initial = jnp.dot(prefix[0], init_gap, precision=highest) + prefix[1]

    def advance(current, pieces):
        step_matrix, step_offset = pieces
        fresh_state = jnp.dot(step_matrix, current, precision=highest) + step_offset
        return (fresh_state, fresh_state)

    _, corrections = lax.scan(advance, initial, (transition, offset))
    updated = jnp.where(active[:, None], next_state + corrections, 0.0)
    defect_out = jnp.where(active[:, None], defect, 0.0)
    return (updated, defect_out)


def solution(mesh):
    in_specs = (
        P(("seg", "block"), None, None),
        P(("seg", "block"), None, None),
        P(("seg", "block"), None, None),
        P(("seg", "block"), None),
        P(("seg", "block"), None),
        P(("seg", "block"), None),
        P(),
        P(),
        P(("seg", "block")),
    )
    out_specs = (P(("seg", "block"), None), P(("seg", "block"), None))
    return jax.shard_map(body, mesh=mesh, in_specs=in_specs, out_specs=out_specs, check_vma=False)
```

profile of v0, /device:TPU:6, one launch (start us, length us, event | category | flops | bytes accessed | tf_op | source)
XLA Modules:
  0.0 121.8 jit_solution(5892687524733374166)
XLA Ops:
  7.2 0.7 slice_bitcast_fusion.5
  8.0 4.9 %collective-permute-start = (f32[128]{0:T(128)S(1)}, f32[128]{0:T(128)S(1)}, u32[]{:S(2)}, u32[]{:S(2)}) collective-permute-start(f32[128]{0:T(128)S(1)} %slice_bitcast_fusion.5), channel_id=1, source_target_pairs={{1,0},{2,1},{3,2},{4,3},{5,4},{6,5},{7,6},{8,7},{9,8},{10,9},{11,1... | collective-permute-start | bytes 1544 | tf_op jit(solution)/shard_map/ppermute | solution.py:12
  13.7 1.5 %fusion.47 = f32[4,128,128]{2,1,0:T(8,128)S(1)} fusion(f32[4,128,128]{2,1,0:T(8,128)} %param.15), kind=kOutput, calls=%fused_computation.69 | convolution fusion | flops 100663296 | bytes 524288 | tf_op jit(solution)/shard_map/kij,kjl->kil/dot_general | solution.py:34
  15.6 0.5 copy-done.1
  16.1 0.5 fusion.35
  16.6 0.4 fusion.23
  17.1 0.3 fusion.30
  17.5 14.9 %all-gather = f32[1024,128]{1,0:T(8,128)S(1)} all-gather(f32[128,128]{1,0:T(8,128)S(1)} %fusion.36), channel_id=2, replica_groups=mesh['seg'=4,'block'=8] {'block'}, dimensions={0}, use_global_device_ids=true | all-gather | bytes 589824 | tf_op jit(solution)/shard_map/all_gather | solution.py:17
  32.5 0.7 copy-done.12
  33.2 0.5 fusion.50
  33.7 0.5 fusion.49
  34.2 0.7 broadcast_select_fusion
  34.9 0.5 fusion.52
  35.5 0.3 fusion.32
  36.1 9.3 %all-gather.1 = f32[8,1,128]{2,1,0:T(1,128)S(1)} all-gather(f32[1,1,128]{2,1,0:T(1,128)S(1)} %bitcast.222), channel_id=1, replica_groups=mesh['seg'=4,'block'=8] {'block'}, dimensions={0}, use_global_device_ids=true | all-gather | bytes 4608 | tf_op jit(solution)/shard_map/all_gather | solution.py:17
  45.4 0.8 fusion.24
  46.4 18.0 %psum.15 = f32[1,128]{1,0:T(1,128)S(1)} all-reduce(f32[1,128]{1,0:T(1,128)S(1)} %fusion.29), channel_id=1, replica_groups=mesh['seg'=4,'block'=8] {'block'}, use_global_device_ids=true, to_apply=%region_3.4 | all-reduce | flops 128 | bytes 1024 | tf_op jit(solution)/shard_map/psum | solution.py:30
  64.4 8.0 %all-gather.2 = f32[4,1,128]{2,1,0:T(1,128)S(1)} all-gather(f32[1,1,128]{2,1,0:T(1,128)S(1)} %bitcast.227), channel_id=1, replica_groups=mesh['seg'=4,'block'=8] {'seg'}, dimensions={0}, use_global_device_ids=true | all-gather | bytes 2560 | tf_op jit(solution)/shard_map/all_gather | solution.py:17
  72.4 29.8 %all-reduce.2.cloned.1.call-done = f32[1,128,128]{2,1,0:T(8,128)} async-done(((f32[1,128,128]{2,1,0:T(8,128)}), f32[1,128,128]{2,1,0:T(8,128)}) %all-reduce.2.cloned.1.call-update) | async-done | bytes 65552 | tf_op jit(solution)/shard_map/psum | solution.py:30
  102.1 8.5 %all_gather.21 = f32[4,128,128]{2,1,0:T(8,128)S(1)} all-gather(f32[1,128,128]{2,1,0:T(8,128)} %all-reduce.2.cloned.1.call-done), channel_id=1, replica_groups=mesh['seg'=4,'block'=8] {'seg'}, dimensions={0}, use_global_device_ids=true | all-gather | bytes 327680 | tf_op jit(solution)/shard_map/all_gather | solution.py:17
  110.6 1.5 %while.40 = (s32[]{:T(128)}, f32[128,128]{1,0:T(8,128)S(1)}, f32[128]{0:T(128)S(1)}, s32[]{:T(128)}, f32[4,128,128]{2,1,0:T(8,128)S(1)}, /*index=5*/f32[4,128]{1,0:T(4,128)S(1)}) while((s32[]{:T(128)}, f32[128,128]{1,0:T(8,128)S(1)}, f32[128]{0:T(128)S(1)}, s32[]{:T(128)}, f32[4,128,128]{2,1,0:T(8,128)S(1)}, ...), condition=%wide.region_5.6_spmd.clone, body=%wide.region_4.5_spmd.sunk.clone | while | flops 25362564 | bytes 396907 | solution.py:25
  112.5 0.5 copy-done.11
  113.2 1.1 while.41
  114.3 0.7 add_select_fusion
  (72 shorter events, 4.3 us)
Async XLA Ops:
  7.2 9.5 %copy-start = (f32[4,128,128]{2,1,0:T(8,128)S(1)}, f32[4,128,128]{2,1,0:T(8,128)}, u32[]{:S(2)}) copy-start(f32[4,128,128]{2,1,0:T(8,128)} %param.16) | copy-start | bytes 786436
  7.2 5.7 %copy-start.8 = (f32[4,128]{1,0:T(4,128)S(1)}, f32[4,128]{1,0:T(4,128)}, u32[]{:S(2)}) copy-start(f32[4,128]{1,0:T(4,128)} %param.20) | copy-start | bytes 6148
  7.2 94.9 %all-reduce.2.cloned.1.call-start = ((), (), s32[]{:S(2)}) async-start(), calls=%async_computation | async-start | bytes 131072 | tf_op jit(solution)/shard_map/psum | solution.py:30
  8.0 24.5 %collective-permute-start = (f32[128]{0:T(128)S(1)}, f32[128]{0:T(128)S(1)}, u32[]{:S(2)}, u32[]{:S(2)}) collective-permute-start(f32[128]{0:T(128)S(1)} %slice_bitcast_fusion.5), channel_id=1, source_target_pairs={{1,0},{2,1},{3,2},{4,3},{5,4},{6,5},{7,6},{8,7},{9,8},{10,9},{11,1... | collective-permute-start | bytes 1544 | tf_op jit(solution)/shard_map/ppermute | solution.py:12
  12.9 3.7 %copy-start.2 = (f32[128,128]{1,0:T(8,128)}, f32[128,128]{1,0:T(8,128)S(1)}, u32[]{:S(2)}) copy-start(f32[128,128]{1,0:T(8,128)S(1)} %fusion.37) | copy-start | bytes 196612
  13.6 1.5 %copy-start.7 = (f32[4,128,64]{1,2,0:T(8,128)S(1)}, f32[4,128,64]{1,2,0:T(8,128)}, u32[]{:S(2)}) copy-start(f32[4,128,64]{1,2,0:T(8,128)} %param.17) | copy-start | bytes 393220
  13.6 1.5 %copy-start.9 = (f32[4,64]{1,0:T(4,128)S(1)}, f32[4,64]{1,0:T(4,128)}, u32[]{:S(2)}) copy-start(f32[4,64]{1,0:T(4,128)} %param.18) | copy-start | bytes 3076
  13.6 1.8 %copy-start.10 = (f32[4,64]{1,0:T(4,128)S(1)}, f32[4,64]{1,0:T(4,128)}, u32[]{:S(2)}) copy-start(f32[4,64]{1,0:T(4,128)} %param.19) | copy-start | bytes 3076
  15.1 1.0 copy-start.1
  32.4 0.7 copy-start.12
  35.9 9.5 %copy-start.6 = (f32[128,128]{1,0:T(8,128)S(1)}, f32[128,128]{1,0:T(8,128)}, u32[]{:S(2)}) copy-start(f32[128,128]{1,0:T(8,128)} %copy-done.2) | copy-start | bytes 196612
  45.4 0.8 copy-start.4
  72.4 38.3 %copy-start.3 = (f32[128,128]{1,0:T(8,128)S(1)}, f32[128,128]{1,0:T(8,128)}, u32[]{:S(2)}) copy-start(f32[128,128]{1,0:T(8,128)} %copy-done.2) | copy-start | bytes 196612
  110.6 1.5 %copy-start.5 = (f32[128,128]{1,0:T(8,128)S(1)}, f32[128,128]{1,0:T(8,128)}, u32[]{:S(2)}) copy-start(f32[128,128]{1,0:T(8,128)} %copy-done.4) | copy-start | bytes 196612
  112.3 0.7 copy-start.11
Sparse Core Ops, SparseCore 0:
  46.4 55.7 all-reduce.1
where the time goes:
time: 124 us; the launch traced here: 122 us
  blocking collectives  58.7 us (47%)
  waiting for transfers between devices  29.8 us (24%)
  between operations  14.9 us (12%)
  matrix products  8.91 us (7%)
  starting transfers between devices  4.95 us (4%)
  local copies, waits for them, and re-layouts  2.85 us (2%)
  other arithmetic  1.51 us (1%)
    all_gather x4, blocking collectives, entering(): gathered = jax.tree.map(lambda a: lax.all_gather(a, axis), part)  40.7 us
    psum x1, waiting for transfers between devices, spread(): return lax.psum(kept, axis)  29.8 us
    psum x1, blocking collectives, spread(): return lax.psum(kept, axis)  18 us
    ppermute x1, starting transfers between devices, from_behind(): return lax.ppermute(value, axis, pairs)  4.91 us
    dot_general x8, matrix products, batch_vector(): return jnp.einsum('kij,kj->ki', matrices, vectors, precision=highest)  3.03 us
  transfers between devices with their start and end apart: 2, of which 1 were waited for; matrix products, arithmetic and copies ran while one was open for 3% of the time, Pallas kernels for 0%

commit v1 on v0

v1 whole, which is shorter than its diff:
```python
import functools
import jax
import jax.numpy as jnp
from jax import lax
from jax.experimental import pallas as pl
from jax.experimental.pallas import tpu as pltpu
from jax.sharding import PartitionSpec as P

MESH = pl.DeviceIdType.MESH
PAD = 8


def halves(x):
    high = x.astype(jnp.bfloat16).astype(jnp.float32)
    return high, x - high


def product(left, right, turned):
    dims = (((1,), (1 if turned else 0,)), ((), ()))
    lh, ll = (h.astype(jnp.bfloat16) for h in halves(left))
    rh, rl = (h.astype(jnp.bfloat16) for h in halves(right))
    rows = jnp.concatenate([lh, ll], axis=1)
    if turned:
        other = jnp.concatenate([rh, rl], axis=0)
        other = jnp.concatenate([other, other], axis=1)
    else:
        other = jnp.concatenate([rh, rl], axis=1)
        other = jnp.concatenate([other, other], axis=0)
    out = lax.dot_general(rows, other, dims, preferred_element_type=jnp.float32)
    width = out.shape[1] // 2
    return out[:, :width] + out[:, width:]


def apply(rows, right, turned):
    count = rows.shape[0]
    dims = (((1,), (1 if turned else 0,)), ((), ()))
    stacked = jnp.concatenate(halves(rows), axis=0).astype(jnp.bfloat16)
    rh, rl = (h.astype(jnp.bfloat16) for h in halves(right))
    other = jnp.concatenate([rh, rl], axis=0 if turned else 1)
    out = lax.dot_general(stacked, other, dims, preferred_element_type=jnp.float32)
    width = out.shape[1] // 2
    out = out[:, :width] + out[:, width:]
    return out[:count] + out[count:]


def kernel(
    segs,
    blocks,
    rounds,
    jac_hbm,
    inv_hbm,
    inp_hbm,
    ctl_ref,
    step_ref,
    traj_ref,
    term_ref,
    gap_ref,
    count_ref,
    upd_ref,
    def_ref,
    jac,
    inv,
    inp,
    first,
    acc,
    got,
    enter,
    maps,
    full,
    vec_in,
    vec_out,
    load_sem,
    first_sem,
    map_send,
    map_recv,
    vec_send,
    vec_recv,
):
    slots, n = traj_ref.shape
    seg = lax.axis_index("seg")
    me = lax.axis_index("block")
    place = seg * blocks + me
    last = segs * blocks - 1
    lead = me == blocks - 1
    passes_on = jnp.logical_and(lead, seg + 1 < segs)

    loads = [
        pltpu.make_async_copy(src, dst, load_sem.at[i])
        for i, (src, dst) in enumerate(((jac_hbm, jac), (inv_hbm, inv), (inp_hbm, inp)))
    ]
    for load in loads:
        load.start()

    barrier = pltpu.get_barrier_semaphore()

    def tell(s, b):
        pl.semaphore_signal(barrier, inc=1, device_id=(s, b), device_id_type=MESH)

    @pl.when(place < last)
    def _():
        tell((place + 1) // blocks, (place + 1) % blocks)

    peers = jnp.where(place > 0, 1, 0)
    for r in range(rounds):
        half = 1 << r

        @pl.when((me // half) % 2 == 1)
        def _():
            tell(seg, (me // half) * half - 1)

        peers += jnp.where(
            me % (2 * half) == half - 1, jnp.minimum(half, blocks - 1 - me), 0
        )

    @pl.when(seg > 0)
    def _():
        tell(seg - 1, blocks - 1)

    peers += jnp.where(passes_on, blocks, 0)

    @pl.when(peers > 0)
    def _():
        pl.semaphore_wait(barrier, peers)

    ahead = jnp.maximum(place - 1, 0)
    first_copy = pltpu.make_async_remote_copy(
        src_ref=traj_ref.at[pl.ds(0, 1)],
        dst_ref=first,
        send_sem=first_sem.at[0],
        recv_sem=first_sem.at[1],
        device_id=(ahead // blocks, ahead % blocks),
        device_id_type=MESH,
    )

    @pl.when(place > 0)
    def _():
        first_copy.start()

    row = lax.broadcasted_iota(jnp.int32, (n, n), 0)
    col = lax.broadcasted_iota(jnp.int32, (n, n), 1)
    eye = jnp.where(row == col, 1.0, 0.0).astype(jnp.float32)
    live = [k < count_ref[0] for k in range(slots)]

    for load in loads:
        load.wait()

    trans = [
        eye + jnp.where(live[k], product(inv[k], jac[k], False), 0.0) for k in range(slots)
    ]
    running = [trans[0].T]
    for k in range(1, slots):
        running.append(product(running[-1], trans[k], True))
    for k in range(slots):
        maps[k, :n] = running[k]

    @pl.when(place < last)
    def _():
        first_copy.wait_recv()

    @pl.when(place == last)
    def _():
        first[...] = term_ref[...]

    upcoming = first[...]

    def eight(x):
        return jnp.broadcast_to(x, (PAD, x.shape[1]))

    nexts, offsets = [], []
    for k in range(slots):
        now = traj_ref[k : k + 1]
        if k + 1 < slots:
            nxt = jnp.where(live[k + 1], traj_ref[k + 1 : k + 2], upcoming)
        else:
            nxt = upcoming
        nexts.append(nxt)
        gap = eight(nxt - now)
        both = jnp.concatenate(
            [ctl_ref[k : k + 1], step_ref[k : k + 1], jnp.zeros((PAD - 2, ctl_ref.shape[1]), jnp.float32)],
            axis=0,
        )
        moved = apply(both, inp[k], True)
        mid = apply(gap, jac[k], True) * (1.0 / 12.0) - eight(0.5 * (nxt + now))
        defect = gap + apply(mid, jac[k], True) - eight(moved[0:1])
        def_ref[k : k + 1] = jnp.where(live[k], defect[0:1], 0.0)
        offset = apply(eight(moved[1:2]) - defect, inv[k], True)
        offsets.append(jnp.where(live[k], offset, 0.0))

    total = offsets[0]
    maps[0, n:] = total
    for k in range(1, slots):
        total = apply(total, trans[k], True) + offsets[k]
        maps[k, n:] = total
    acc[...] = maps[slots - 1]

    def compose(early, late):
        zeros = jnp.zeros((PAD, n), jnp.float32)
        rows = product(jnp.concatenate([early, zeros], axis=0), late[:n], False)
        tail = rows[n : n + PAD] + late[n:]
        return jnp.concatenate([rows[:n], tail], axis=0)

    def map_copy(r, to, j):
        return pltpu.make_async_remote_copy(
            src_ref=acc,
            dst_ref=got.at[r],
            send_sem=map_send.at[j],
            recv_sem=map_recv.at[r],
            device_id=(seg, to),
            device_id_type=MESH,
        )

    for r in range(rounds):
        half = 1 << r

        @pl.when(me % (2 * half) == half - 1)
        def _():
            for j in range(half, 0, -1):

                @pl.when(me + j < blocks)
                def _():
                    map_copy(r, me + j, j - 1).start()

        needed = jnp.logical_or(me % (2 * half) == 2 * half - 1, lead)

        @pl.when(jnp.logical_and(needed, (me // half) % 2 == 1))
        def _():
            map_copy(r, me, 0).wait_recv()
            acc[...] = compose(got[r], acc[...])

    def vec_copy(to):
        return pltpu.make_async_remote_copy(
            src_ref=vec_out,
            dst_ref=vec_in,
            send_sem=vec_send.at[to],
            recv_sem=vec_recv,
            device_id=(jnp.minimum(seg + 1, segs - 1), to),
            device_id_type=MESH,
        )

    @pl.when(seg == 0)
    def _():
        vec_in[...] = eight(gap_ref[...])

    @pl.when(passes_on)
    def _():
        @pl.when(seg > 0)
        def _():
            vec_copy(0).wait_recv()

        vec_out[...] = apply(vec_in[...], acc[:n], False) + acc[n:]
        for j in range(blocks - 1, -1, -1):
            vec_copy(j).start()

    enter[:n] = eye
    enter[n:] = jnp.zeros((PAD, n), jnp.float32)
    for r in reversed(range(rounds)):
        half = 1 << r
        bit = (me // half) % 2 == 1
        needed = jnp.logical_or(me % (2 * half) == 2 * half - 1, lead)

        @pl.when(jnp.logical_and(bit, jnp.logical_not(needed)))
        def _():
            map_copy(r, me, 0).wait_recv()

        @pl.when(bit)
        def _():
            enter[...] = compose(enter[...], got[r])

    start = enter[...]
    for k in range(slots):
        full[k] = compose(start, maps[k])

    @pl.when(jnp.logical_and(seg > 0, jnp.logical_not(passes_on)))
    def _():
        vec_copy(0).wait_recv()

    vec = vec_in[...]
    for k in range(slots):
        after = apply(vec, full[k, :n], False) + full[k, n:]
        upd_ref[k : k + 1] = jnp.where(live[k], nexts[k] + after[0:1], 0.0)

    @pl.when(place > 0)
    def _():
        first_copy.wait_send()

    for r in range(rounds):
        half = 1 << r

        @pl.when(me % (2 * half) == half - 1)
        def _():
            for j in range(half, 0, -1):

                @pl.when(me + j < blocks)
                def _():
                    map_copy(r, me + j, j - 1).wait_send()

    @pl.when(passes_on)
    def _():
        for j in range(blocks - 1, -1, -1):
            vec_copy(j).wait_send()


def body(
    jacobian,
    implicit_inv,
    input_map,
    controls,
    control_step,
    state_traj,
    terminal,
    init_gap,
    counts,
):
    segs, blocks = lax.axis_size("seg"), lax.axis_size("block")
    slots, n = state_traj.shape
    rounds = max(blocks - 1, 0).bit_length()
    anywhere = pl.BlockSpec(memory_space=pl.ANY)
    vmem = pl.BlockSpec(memory_space=pltpu.VMEM)
    smem = pl.BlockSpec(memory_space=pltpu.SMEM)
    f32 = jnp.float32
    shape = jax.ShapeDtypeStruct((slots, n), f32)
    return pl.pallas_call(
        functools.partial(kernel, segs, blocks, rounds),
        out_shape=(shape, shape),
        in_specs=[anywhere] * 3 + [vmem] * 5 + [smem],
        out_specs=(vmem, vmem),
        scratch_shapes=[
            pltpu.VMEM(jacobian.shape, f32),
            pltpu.VMEM(implicit_inv.shape, f32),
            pltpu.VMEM(input_map.shape, f32),
            pltpu.VMEM((1, n), f32),
            pltpu.VMEM((n + PAD, n), f32),
            pltpu.VMEM((max(rounds, 1), n + PAD, n), f32),
            pltpu.VMEM((n + PAD, n), f32),
            pltpu.VMEM((slots, n + PAD, n), f32),
            pltpu.VMEM((slots, n + PAD, n), f32),
            pltpu.VMEM((PAD, n), f32),
            pltpu.VMEM((PAD, n), f32),
            pltpu.SemaphoreType.DMA((3,)),
            pltpu.SemaphoreType.DMA((2,)),
            pltpu.SemaphoreType.DMA((blocks,)),
            pltpu.SemaphoreType.DMA((max(rounds, 1),)),
            pltpu.SemaphoreType.DMA((blocks,)),
            pltpu.SemaphoreType.DMA,
        ],
        compiler_params=pltpu.CompilerParams(
            collective_id=0, has_side_effects=True, vmem_limit_bytes=24 * 1024 * 1024
        ),
    )(
        jacobian,
        implicit_inv,
        input_map,
        controls,
        control_step,
        state_traj,
        terminal[None],
        init_gap[None],
        counts,
    )


def solution(mesh):
    in_specs = (
        P(("seg", "block"), None, None),
        P(("seg", "block"), None, None),
        P(("seg", "block"), None, None),
        P(("seg", "block"), None),
        P(("seg", "block"), None),
        P(("seg", "block"), None),
        P(),
        P(),
        P(("seg", "block")),
    )
    out_specs = (P(("seg", "block"), None), P(("seg", "block"), None))
    return jax.shard_map(body, mesh=mesh, in_specs=in_specs, out_specs=out_specs, check_vma=False)
```

time: 124 us -> 23.3 us (0.19); the launches traced: 122 us -> 23.1 us
  blocking collectives: 58.7 us -> 0 us
  waiting for transfers between devices: 29.8 us -> 0 us
  Pallas kernels: 0 us -> 18.5 us
  between operations: 14.9 us -> 1.44 us
  matrix products: 8.91 us -> 0 us
  starting transfers between devices: 4.95 us -> 0 us
  other arithmetic: 1.51 us -> 0 us
    all_gather x4 -> x0, blocking collectives: 40.7 us -> none  [entering(): gathered = jax.tree.map(lambda a: lax.all_gather(a, axis), part)]
    psum x1 -> x0, waiting for transfers between devices: 29.8 us -> none  [spread(): return lax.psum(kept, axis)]
    pallas_call x0 -> x1, Pallas kernels: none -> 18.5 us  [body(): pl.pallas_call(functools.partial(kernel, segs, blocks, rounds), out_shape...]
    psum x1 -> x0, blocking collectives: 18 us -> none  [spread(): return lax.psum(kept, axis)]
    dot_general x27 -> x0, matrix products: 8.91 us -> none  [the longest x8 3.03 us: batch_vector(): return jnp.einsum('kij,kj->ki', matrices, vectors, precision=highest)]
    ppermute x1 -> x0, starting transfers between devices: 4.91 us -> none  [from_behind(): return lax.ppermute(value, axis, pairs)]
    unnamed x26 -> x17, local copies, waits for them, and re-layouts: 1.64 us -> 3.19 us
    select_n x5 -> x0, other arithmetic: 1.48 us -> none  [the longest x1 0.67 us: body(): defect_out = jnp.where(active[:, None], defect, 0.0)]
  transfers between devices with their start and end apart: 2 -> 0, of which waited for: 1 -> 0; matrix products, arithmetic and copies ran while one was open for 3% -> 0% of each run, Pallas kernels for 0% -> 0%
where the time goes in v1:
time: 23.3 us; the launch traced here: 23.1 us
  Pallas kernels  18.5 us (79%)
  local copies, waits for them, and re-layouts  3.19 us (14%)
  between operations  1.44 us (6%)
    pallas_call x1, Pallas kernels, body(): pl.pallas_call(functools.partial(kernel, segs, blocks, rounds), out_shape...  18.5 us
    unnamed x17, local copies, waits for them, and re-layouts  3.19 us

profile of v1, /device:TPU:6, one launch (start us, length us, event | category | flops | bytes accessed | tf_op | source)
XLA Modules:
  0.0 23.1 jit_solution(2075219290563779438)
XLA Ops:
  0.6 0.0 copy-start
  1.3 0.0 copy-start.2
  1.3 0.0 copy-start.3
  1.4 0.0 copy-start.4
  1.4 0.0 copy-start.5
  1.4 0.0 copy-start.6
  1.4 1.1 %copy.11.inp_hbm = f32[4,128,64]{2,1,0:T(8,128)S(1)} copy(f32[4,128,64]{1,2,0:T(8,128)} %param.11) | data formatting | bytes 262144 | tf_op args[2]
  2.4 0.0 copy-done
  2.5 0.0 copy-done.2
  2.5 0.0 copy-done.3
  2.5 0.0 copy-done.4
  2.5 0.0 copy-done.5
  2.5 0.0 copy-done.6
  2.5 0.0 copy-start.1
  2.5 0.9 %copy-done.1 = f32[4,128,128]{2,1,0:T(8,128)S(1)} copy-done((f32[4,128,128]{2,1,0:T(8,128)S(1)}, f32[4,128,128]{2,1,0:T(8,128)}, u32[]{:S(2)}) %copy-start.1) | copy-done | bytes 262168
  3.5 18.5 %shard_map.104 = (f32[4,128]{1,0:T(4,128)S(1)}, f32[4,128]{1,0:T(4,128)S(1)}) custom-call(f32[4,128,128]{2,1,0:T(8,128)S(1)} %copy-done, f32[4,128,128]{2,1,0:T(8,128)S(1)} %copy-done.1, f32[4,128,64]{2,1,0:T(8,128)S(1)} %copy.11.inp_hbm, f32[4,64]{1,0:T(4,128)S(1)} %copy-done.2, f32[4,64]{1,0:T(4,128)S(1)} %copy-done.3, f32[4,128]{1,0:T(4,128)S(1)} %copy-done.4, ...), custom_call_target="tpu_custom_call" | custom-call | tf_op jit(solution)/shard_map/pallas_call | solution.py:322
  21.9 0.6 %copy.15 = f32[4,128]{1,0:T(4,128)} copy(f32[4,128]{1,0:T(4,128)S(1)} %get-tuple-element.4) | data formatting | bytes 4096
  22.5 0.6 %copy.16 = f32[4,128]{1,0:T(4,128)} copy(f32[4,128]{1,0:T(4,128)S(1)} %get-tuple-element.5) | data formatting | bytes 4096
Async XLA Ops:
  0.6 1.8 %copy-start = (f32[4,128,128]{2,1,0:T(8,128)S(1)}, f32[4,128,128]{2,1,0:T(8,128)}, u32[]{:S(2)}) copy-start(f32[4,128,128]{2,1,0:T(8,128)} %jac_hbm.1) | copy-start | bytes 786436
  1.3 1.1 %copy-start.2 = (f32[4,64]{1,0:T(4,128)S(1)}, f32[4,64]{1,0:T(4,128)}, u32[]{:S(2)}) copy-start(f32[4,64]{1,0:T(4,128)} %ctl_ref.1) | copy-start | bytes 3076
  1.3 1.1 %copy-start.3 = (f32[4,64]{1,0:T(4,128)S(1)}, f32[4,64]{1,0:T(4,128)}, u32[]{:S(2)}) copy-start(f32[4,64]{1,0:T(4,128)} %step_ref.1) | copy-start | bytes 3076
  1.4 1.1 %copy-start.4 = (f32[4,128]{1,0:T(4,128)S(1)}, f32[4,128]{1,0:T(4,128)}, u32[]{:S(2)}) copy-start(f32[4,128]{1,0:T(4,128)} %traj_ref.1) | copy-start | bytes 6148
  1.4 1.1 %copy-start.5 = (f32[128]{0:T(128)S(1)}, f32[128]{0:T(128)}, u32[]{:S(2)}) copy-start(f32[128]{0:T(128)} %param.15) | copy-start | bytes 1540
  1.4 1.1 %copy-start.6 = (f32[128]{0:T(128)S(1)}, f32[128]{0:T(128)}, u32[]{:S(2)}) copy-start(f32[128]{0:T(128)} %param.16) | copy-start | bytes 1540
  2.5 1.0 %copy-start.1 = (f32[4,128,128]{2,1,0:T(8,128)S(1)}, f32[4,128,128]{2,1,0:T(8,128)}, u32[]{:S(2)}) copy-start(f32[4,128,128]{2,1,0:T(8,128)} %inv_hbm.1) | copy-start | bytes 786436

commit v2 on v1

v2 whole, which is shorter than its diff:
```python
import functools
import jax
import jax.numpy as jnp
from jax import lax
from jax.experimental import pallas as pl
from jax.experimental.pallas import tpu as pltpu
from jax.sharding import PartitionSpec as P

MESH = pl.DeviceIdType.MESH
PAD = 8


def halves(x):
    high = x.astype(jnp.bfloat16).astype(jnp.float32)
    return high, x - high


def product(left, right, turned):
    dims = (((1,), (1 if turned else 0,)), ((), ()))
    lh, ll = (h.astype(jnp.bfloat16) for h in halves(left))
    rh, rl = (h.astype(jnp.bfloat16) for h in halves(right))
    rows = jnp.concatenate([lh, ll], axis=1)
    if turned:
        other = jnp.concatenate([rh, rl], axis=0)
        other = jnp.concatenate([other, other], axis=1)
    else:
        other = jnp.concatenate([rh, rl], axis=1)
        other = jnp.concatenate([other, other], axis=0)
    out = lax.dot_general(rows, other, dims, preferred_element_type=jnp.float32)
    width = out.shape[1] // 2
    return out[:, :width] + out[:, width:]


def apply(rows, right, turned):
    count = rows.shape[0]
    dims = (((1,), (1 if turned else 0,)), ((), ()))
    stacked = jnp.concatenate(halves(rows), axis=0).astype(jnp.bfloat16)
    rh, rl = (h.astype(jnp.bfloat16) for h in halves(right))
    other = jnp.concatenate([rh, rl], axis=0 if turned else 1)
    out = lax.dot_general(stacked, other, dims, preferred_element_type=jnp.float32)
    width = out.shape[1] // 2
    out = out[:, :width] + out[:, width:]
    return out[:count] + out[count:]


def compose(early, late):
    n = late.shape[1]
    zeros = jnp.zeros((PAD, n), jnp.float32)
    rows = product(jnp.concatenate([early, zeros], axis=0), late[:n], False)
    tail = rows[n : n + PAD] + late[n:]
    return jnp.concatenate([rows[:n], tail], axis=0)


def kernel(
    segs,
    blocks,
    rounds,
    jac_hbm,
    inv_hbm,
    inp_hbm,
    ctl_hbm,
    step_hbm,
    traj_hbm,
    term_hbm,
    gap_hbm,
    count_hbm,
    out_ref,
    jac,
    inv,
    inp,
    ctl,
    step,
    traj,
    term,
    gap,
    count,
    first,
    acc,
    got,
    enter,
    maps,
    full,
    vec_in,
    vec_out,
    load_sem,
    first_sem,
    map_send,
    map_recv,
    vec_send,
    vec_recv,
):
    slots, n = traj.shape
    seg = lax.axis_index("seg")
    me = lax.axis_index("block")
    place = seg * blocks + me
    last = segs * blocks - 1
    odd = me % 2 == 1
    even = me % 2 == 0
    mate = me + 1 - 2 * (me % 2)
    passes_on = jnp.logical_and(odd, seg + 1 < segs)

    loads = [
        pltpu.make_async_copy(src, dst, load_sem.at[i])
        for i, (src, dst) in enumerate(
            (
                (traj_hbm, traj),
                (count_hbm, count),
                (jac_hbm, jac),
                (inv_hbm, inv),
                (inp_hbm, inp),
                (ctl_hbm, ctl),
                (step_hbm, step),
                (term_hbm, term),
                (gap_hbm, gap),
            )
        )
    ]
    for load in loads:
        load.start()

    barrier = pltpu.get_barrier_semaphore()

    def tell(s, b):
        pl.semaphore_signal(barrier, inc=1, device_id=(s, b), device_id_type=MESH)

    def partner(r):
        half = 1 << r
        return me + half - 2 * half * ((me // half) % 2)

    tell(seg, mate)

    @pl.when(place < last)
    def _():
        tell((place + 1) // blocks, (place + 1) % blocks)

    @pl.when(odd)
    def _():
        for r in range(1, rounds):
            tell(seg, partner(r))

    @pl.when(seg > 0)
    def _():
        tell(seg - 1, me + 1 - me % 2)

    peers = 1 + jnp.where(place > 0, 1, 0) + jnp.where(odd, rounds - 1, 0)
    peers += jnp.where(passes_on, 2, 0)
    pl.semaphore_wait(barrier, peers)

    ahead = jnp.maximum(place - 1, 0)
    first_copy = pltpu.make_async_remote_copy(
        src_ref=traj.at[pl.ds(0, 1)],
        dst_ref=first,
        send_sem=first_sem.at[0],
        recv_sem=first_sem.at[1],
        device_id=(ahead // blocks, ahead % blocks),
        device_id_type=MESH,
    )
    loads[0].wait()

    @pl.when(place > 0)
    def _():
        first_copy.start()

    row = lax.broadcasted_iota(jnp.int32, (n, n), 0)
    col = lax.broadcasted_iota(jnp.int32, (n, n), 1)
    eye = jnp.where(row == col, 1.0, 0.0).astype(jnp.float32)
    for load in loads[1:]:
        load.wait()
    live = [k < count[0] for k in range(slots)]

    trans = [
        eye + jnp.where(live[k], product(inv[k], jac[k], False), 0.0) for k in range(slots)
    ]
    known = {}

    def fold(lo, hi):
        if (lo, hi) not in known:
            if hi - lo == 1:
                known[lo, hi] = trans[lo].T
            else:
                mid = (lo + hi) // 2 if lo or hi == slots else hi - 1
                early = fold(lo, mid)
                if hi - mid == 1:
                    known[lo, hi] = product(early, trans[mid], True)
                else:
                    known[lo, hi] = product(early, fold(mid, hi), False)
        return known[lo, hi]

    acc[0, :n] = fold(0, slots)

    @pl.when(place < last)
    def _():
        first_copy.wait_recv()

    @pl.when(place == last)
    def _():
        first[...] = term[...]

    upcoming = first[...]

    def eight(x):
        return jnp.broadcast_to(x, (PAD, x.shape[1]))

    nexts, offsets = [], []
    for k in range(slots):
        now = traj[k : k + 1]
        if k + 1 < slots:
            nxt = jnp.where(live[k + 1], traj[k + 1 : k + 2], upcoming)
        else:
            nxt = upcoming
        nexts.append(nxt)
        change = eight(nxt - now)
        both = jnp.concatenate(
            [ctl[k : k + 1], step[k : k + 1], jnp.zeros((PAD - 2, ctl.shape[1]), jnp.float32)],
            axis=0,
        )
        moved = apply(both, inp[k], False)
        mid = apply(change, jac[k], True) * (1.0 / 12.0) - eight(0.5 * (nxt + now))
        defect = change + apply(mid, jac[k], True) - eight(moved[0:1])
        out_ref[1, k : k + 1] = jnp.where(live[k], defect[0:1], 0.0)
        offset = apply(eight(moved[1:2]) - defect, inv[k], True)
        offsets.append(jnp.where(live[k], offset, 0.0))
    known_vec = {}

    def fold_vec(lo, hi):
        if (lo, hi) not in known_vec:
            if hi - lo == 1:
                known_vec[lo, hi] = offsets[lo]
            else:
                mid = (lo + hi) // 2 if lo or hi == slots else hi - 1
                early = fold_vec(lo, mid)
                if hi - mid == 1:
                    moved = apply(early, trans[mid], True)
                else:
                    moved = apply(early, fold(mid, hi), False)
                known_vec[lo, hi] = moved + fold_vec(mid, hi)
        return known_vec[lo, hi]

    acc[0, n:] = fold_vec(0, slots)

    def map_copy(src, r, to):
        return pltpu.make_async_remote_copy(
            src_ref=src,
            dst_ref=got.at[r],
            send_sem=map_send.at[r],
            recv_sem=map_recv.at[r],
            device_id=(seg, to),
            device_id_type=MESH,
        )

    @pl.when(even)
    def _():
        map_copy(acc.at[0], 0, mate).start()

    for k in range(slots):
        maps[k, :n] = fold(0, k + 1)
        maps[k, n:] = fold_vec(0, k + 1)

    @pl.when(odd)
    def _():
        map_copy(acc.at[0], 0, mate).wait_recv()
        acc[1] = compose(got[0], acc[0])
        for r in range(1, rounds):
            map_copy(acc.at[r], r, partner(r)).start()
            if r == 1:
                enter[:n] = eye
                enter[n:] = jnp.zeros((PAD, n), jnp.float32)
            map_copy(acc.at[r], r, partner(r)).wait_recv()
            high = (me // (1 << r)) % 2 == 1

            @pl.when(high)
            def _():
                acc[r + 1] = compose(got[r], acc[r])
                enter[...] = compose(got[r], enter[...])

            @pl.when(jnp.logical_not(high))
            def _():
                acc[r + 1] = compose(acc[r], got[r])

        map_copy(enter, rounds, mate).start()

    def vec_copy(i):
        return pltpu.make_async_remote_copy(
            src_ref=vec_out,
            dst_ref=vec_in,
            send_sem=vec_send.at[i],
            recv_sem=vec_recv,
            device_id=(jnp.minimum(seg + 1, segs - 1), me + 1 - me % 2 - i),
            device_id_type=MESH,
        )

    @pl.when(seg == 0)
    def _():
        vec_in[...] = eight(gap[...])

    @pl.when(passes_on)
    def _():
        @pl.when(seg > 0)
        def _():
            vec_copy(0).wait_recv()

        vec_out[...] = apply(vec_in[...], acc[rounds, :n], False) + acc[rounds, n:]
        for i in range(2):
            vec_copy(i).start()

    @pl.when(even)
    def _():
        map_copy(enter, rounds, mate).wait_recv()
        start = got[rounds]
        for k in range(slots):
            full[k] = compose(start, maps[k])

    @pl.when(odd)
    def _():
        start = compose(enter[...], got[0])
        for k in range(slots):
            full[k] = compose(start, maps[k])

    @pl.when(jnp.logical_and(seg > 0, jnp.logical_not(passes_on)))
    def _():
        vec_copy(0).wait_recv()

    vec = vec_in[...]
    for k in range(slots):
        after = apply(vec, full[k, :n], False) + full[k, n:]
        out_ref[0, k : k + 1] = jnp.where(live[k], nexts[k] + after[0:1], 0.0)

    @pl.when(place > 0)
    def _():
        first_copy.wait_send()

    @pl.when(even)
    def _():
        map_copy(acc.at[0], 0, mate).wait_send()

    @pl.when(odd)
    def _():
        for r in range(1, rounds):
            map_copy(acc.at[r], r, partner(r)).wait_send()
        map_copy(enter, rounds, mate).wait_send()

    @pl.when(passes_on)
    def _():
        for i in range(2):
            vec_copy(i).wait_send()


def body(
    jacobian,
    implicit_inv,
    input_map,
    controls,
    control_step,
    state_traj,
    terminal,
    init_gap,
    counts,
):
    segs, blocks = lax.axis_size("seg"), lax.axis_size("block")
    slots, n = state_traj.shape
    rounds = blocks.bit_length() - 1
    if blocks < 4 or blocks != 1 << rounds:
        raise ValueError("blocks")
    f32 = jnp.float32
    operands = (
        jacobian,
        implicit_inv,
        jnp.swapaxes(input_map, 1, 2),
        controls,
        control_step,
        state_traj,
        terminal[None],
        init_gap[None],
        counts,
    )
    out = pl.pallas_call(
        functools.partial(kernel, segs, blocks, rounds),
        out_shape=jax.ShapeDtypeStruct((2, slots, n), f32),
        in_specs=[pl.BlockSpec(memory_space=pltpu.HBM)] * len(operands),
        out_specs=pl.BlockSpec(memory_space=pltpu.VMEM),
        scratch_shapes=[pltpu.VMEM(x.shape, f32) for x in operands[:-1]]
        + [
            pltpu.SMEM(counts.shape, jnp.int32),
            pltpu.VMEM((1, n), f32),
            pltpu.VMEM((rounds + 1, n + PAD, n), f32),
            pltpu.VMEM((rounds + 1, n + PAD, n), f32),
            pltpu.VMEM((n + PAD, n), f32),
            pltpu.VMEM((slots, n + PAD, n), f32),
            pltpu.VMEM((slots, n + PAD, n), f32),
            pltpu.VMEM((PAD, n), f32),
            pltpu.VMEM((PAD, n), f32),
            pltpu.SemaphoreType.DMA((len(operands),)),
            pltpu.SemaphoreType.DMA((2,)),
            pltpu.SemaphoreType.DMA((rounds + 1,)),
            pltpu.SemaphoreType.DMA((rounds + 1,)),
            pltpu.SemaphoreType.DMA((2,)),
            pltpu.SemaphoreType.DMA,
        ],
        compiler_params=pltpu.CompilerParams(
            collective_id=0, has_side_effects=True, vmem_limit_bytes=60 * 1024 * 1024
        ),
    )(*operands)
    return out[0], out[1]


def solution(mesh):
    in_specs = (
        P(("seg", "block"), None, None),
        P(("seg", "block"), None, None),
        P(("seg", "block"), None, None),
        P(("seg", "block"), None),
        P(("seg", "block"), None),
        P(("seg", "block"), None),
        P(),
        P(),
        P(("seg", "block")),
    )
    out_specs = (P(("seg", "block"), None), P(("seg", "block"), None))
    return jax.shard_map(body, mesh=mesh, in_specs=in_specs, out_specs=out_specs, check_vma=False)
```

time: 23.3 us -> 23.1 us (level)
  local copies, waits for them, and re-layouts: 3.19 us -> 1.26 us
  Pallas kernels: 18.5 us -> 20.4 us
    unnamed x17 -> x0, local copies, waits for them, and re-layouts: 3.19 us -> none
    pallas_call x1, Pallas kernels: 18.5 us -> 20.4 us  [body(): pl.pallas_call(functools.partial(kernel, segs, blocks, rounds), out_shape...]
    squeeze x0 -> x1, local copies, waits for them, and re-layouts: none -> 1.26 us  [body(): return (out[0], out[1])]
where the time goes in v2:
time: 23.1 us; the launch traced here: 22.9 us
  Pallas kernels  20.4 us (88%)
  between operations  1.29 us (6%)
  local copies, waits for them, and re-layouts  1.26 us (5%)
    pallas_call x1, Pallas kernels, body(): pl.pallas_call(functools.partial(kernel, segs, blocks, rounds), out_shape...  20.4 us
    squeeze x1, local copies, waits for them, and re-layouts, body(): return (out[0], out[1])  1.26 us

profile of v2, /device:TPU:6, one launch (start us, length us, event | category | flops | bytes accessed | tf_op | source)
XLA Modules:
  0.0 22.9 jit_solution(11181550575412850484)
XLA Ops:
  1.3 20.4 %shard_map.104 = f32[2,4,128]{2,1,0:T(4,128)} custom-call(f32[4,128,128]{2,1,0:T(8,128)} %jac_hbm.1, f32[4,128,128]{2,1,0:T(8,128)} %inv_hbm.1, f32[4,64,128]{2,1,0:T(8,128)} %bitcast.7, f32[4,64]{1,0:T(4,128)} %ctl_hbm.1, f32[4,64]{1,0:T(4,128)} %step_hbm.1, f32[4,128]{1,0:T(4,128)} %traj_hbm.1, f32[1,128]{1,0:T(1,128)} %bitcast.8, f32[1,128]{1,0:T(1,128)} %bitcast.9, ...), custom_call_target="tpu_custom_call" | custom-call | tf_op jit(solution)/shard_map/pallas_call | solution.py:376
  21.6 1.3 %slice_bitcast_fusion = (f32[4,128]{1,0:T(4,128)}, f32[4,128]{1,0:T(4,128)}) fusion(f32[2,4,128]{2,1,0:T(4,128)} %shard_map.104), kind=kLoop, calls=%fused_computation | loop fusion | bytes 8192 | tf_op jit(solution)/shard_map/squeeze | solution.py:403

commit v3 on v2

--- a/solution.py
+++ b/solution.py
@@ -80,6 +80,7 @@
     enter,
     maps,
     full,
+    tails,
     vec_in,
     vec_out,
     load_sem,
@@ -94,10 +95,7 @@
     me = lax.axis_index("block")
     place = seg * blocks + me
     last = segs * blocks - 1
-    odd = me % 2 == 1
-    even = me % 2 == 0
-    mate = me + 1 - 2 * (me % 2)
-    passes_on = jnp.logical_and(odd, seg + 1 < segs)
+    passes_on = jnp.logical_and(me == blocks - 1, seg + 1 < segs)
 
     loads = [
         pltpu.make_async_copy(src, dst, load_sem.at[i])
@@ -123,27 +121,25 @@
     def tell(s, b):
         pl.semaphore_signal(barrier, inc=1, device_id=(s, b), device_id_type=MESH)
 
-    def partner(r):
+    @pl.when(place < last)
+    def _():
+        tell((place + 1) // blocks, (place + 1) % blocks)
+
+    peers = jnp.where(place > 0, 1, 0)
+    for r in range(rounds):
         half = 1 << r
-        return me + half - 2 * half * ((me // half) % 2)
-
-    tell(seg, mate)
-
-    @pl.when(place < last)
-    def _():
-        tell((place + 1) // blocks, (place + 1) % blocks)
-
-    @pl.when(odd)
-    def _():
-        for r in range(1, rounds):
-            tell(seg, partner(r))
+
+        @pl.when((me // half) % 2 == 1)
+        def _():
+            tell(seg, (me // half) * half - 1)
+
+        peers += jnp.where(me % (2 * half) == half - 1, half, 0)
 
     @pl.when(seg > 0)
     def _():
-        tell(seg - 1, me + 1 - me % 2)
-
-    peers = 1 + jnp.where(place > 0, 1, 0) + jnp.where(odd, rounds - 1, 0)
-    peers += jnp.where(passes_on, 2, 0)
+        tell(seg - 1, blocks - 1)
+
+    peers += jnp.where(passes_on, blocks, 0)
     pl.semaphore_wait(barrier, peers)
 
     ahead = jnp.maximum(place - 1, 0)
@@ -167,6 +163,14 @@
     for load in loads[1:]:
         load.wait()
     live = [k < count[0] for k in range(slots)]
+
+    @pl.when(place < last)
+    def _():
+        first_copy.wait_recv()
+
+    @pl.when(place == last)
+    def _():
+        first[...] = term[...]
 
     trans = [
         eye + jnp.where(live[k], product(inv[k], jac[k], False), 0.0) for k in range(slots)
@@ -186,15 +190,7 @@
                     known[lo, hi] = product(early, fold(mid, hi), False)
         return known[lo, hi]
 
-    acc[0, :n] = fold(0, slots)
-
-    @pl.when(place < last)
-    def _():
-        first_copy.wait_recv()
-
-    @pl.when(place == last)
-    def _():
-        first[...] = term[...]
+    acc[:n] = fold(0, slots)
 
     upcoming = first[...]
 
@@ -236,56 +232,62 @@
                 known_vec[lo, hi] = moved + fold_vec(mid, hi)
         return known_vec[lo, hi]
 
-    acc[0, n:] = fold_vec(0, slots)
-
-    def map_copy(src, r, to):
+    acc[n:] = fold_vec(0, slots)
+
+    def map_copy(r, to, j):
         return pltpu.make_async_remote_copy(
-            src_ref=src,
+            src_ref=acc,
             dst_ref=got.at[r],
-            send_sem=map_send.at[r],
+            send_sem=map_send.at[j],
             recv_sem=map_recv.at[r],
             device_id=(seg, to),
             device_id_type=MESH,
         )
 
-    @pl.when(even)
-    def _():
-        map_copy(acc.at[0], 0, mate).start()
+    for r in range(rounds):
+        half = 1 << r
+
+        @pl.when(me % (2 * half) == half - 1)
+        def _():
+            for j in range(half, 0, -1):
+                map_copy(r, me + j, j - 1).start()
+
+        @pl.when(jnp.logical_and(me % (2 * half) == 2 * half - 1, me < blocks - 1))
+        def _():
+            map_copy(r, me, 0).wait_recv()
+            acc[...] = compose(got[r], acc[...])
 
     for k in range(slots):
         maps[k, :n] = fold(0, k + 1)
         maps[k, n:] = fold_vec(0, k + 1)
 
-    @pl.when(odd)
-    def _():
-        map_copy(acc.at[0], 0, mate).wait_recv()
-        acc[1] = compose(got[0], acc[0])
-        for r in range(1, rounds):
-            map_copy(acc.at[r], r, partner(r)).start()
-            if r == 1:
-                enter[:n] = eye
-                enter[n:] = jnp.zeros((PAD, n), jnp.float32)
-            map_copy(acc.at[r], r, partner(r)).wait_recv()
-            high = (me // (1 << r)) % 2 == 1
-
-            @pl.when(high)
+    enter[:n] = eye
+    enter[n:] = jnp.zeros((PAD, n), jnp.float32)
+    for r in reversed(range(rounds)):
+        half = 1 << r
+        done = jnp.logical_and(me % (2 * half) == 2 * half - 1, me < blocks - 1)
+
+        @pl.when((me // half) % 2 == 1)
+        def _():
+            @pl.when(jnp.logical_not(done))
             def _():
-                acc[r + 1] = compose(got[r], acc[r])
-                enter[...] = compose(got[r], enter[...])
-
-            @pl.when(jnp.logical_not(high))
-            def _():
-                acc[r + 1] = compose(acc[r], got[r])
-
-        map_copy(enter, rounds, mate).start()
-
-    def vec_copy(i):
+                map_copy(r, me, 0).wait_recv()
+
+            enter[...] = compose(enter[...], got[r])
+
+    start = enter[...]
+    for k in reversed(range(slots)):
+        rows = compose(start, maps[k])
+        full[k] = jnp.concatenate(halves(rows[:n]), axis=1).astype(jnp.bfloat16)
+        tails[k] = rows[n:]
+
+    def vec_copy(to):
         return pltpu.make_async_remote_copy(
             src_ref=vec_out,
             dst_ref=vec_in,
-            send_sem=vec_send.at[i],
+            send_sem=vec_send.at[to],
             recv_sem=vec_recv,
-            device_id=(jnp.minimum(seg + 1, segs - 1), me + 1 - me % 2 - i),
+            device_id=(jnp.minimum(seg + 1, segs - 1), to),
             device_id_type=MESH,
         )
 
@@ -293,56 +295,42 @@
     def _():
         vec_in[...] = eight(gap[...])
 
+    @pl.when(seg > 0)
+    def _():
+        vec_copy(0).wait_recv()
+
+    stacked = jnp.concatenate(halves(vec_in[...]), axis=0).astype(jnp.bfloat16)
+
+    def after(k):
+        rows = jnp.dot(stacked, full[k], preferred_element_type=jnp.float32)
+        rows = rows[:, :n] + rows[:, n:]
+        return rows[:PAD] + rows[PAD:] + tails[k]
+
     @pl.when(passes_on)
     def _():
-        @pl.when(seg > 0)
+        vec_out[...] = after(slots - 1)
+        for to in range(blocks - 1, -1, -1):
+            vec_copy(to).start()
+
+    for k in range(slots):
+        out_ref[0, k : k + 1] = jnp.where(live[k], nexts[k] + after(k)[0:1], 0.0)
+
+    @pl.when(place > 0)
+    def _():
+        first_copy.wait_send()
+
+    for r in range(rounds):
+        half = 1 << r
+
+        @pl.when(me % (2 * half) == half - 1)
         def _():
-            vec_copy(0).wait_recv()
-
-        vec_out[...] = apply(vec_in[...], acc[rounds, :n], False) + acc[rounds, n:]
-        for i in range(2):
-            vec_copy(i).start()
-
-    @pl.when(even)
-    def _():
-        map_copy(enter, rounds, mate).wait_recv()
-        start = got[rounds]
-        for k in range(slots):
-            full[k] = compose(start, maps[k])
-
-    @pl.when(odd)
-    def _():
-        start = compose(enter[...], got[0])
-        for k in range(slots):
-            full[k] = compose(start, maps[k])
-
-    @pl.when(jnp.logical_and(seg > 0, jnp.logical_not(passes_on)))
-    def _():
-        vec_copy(0).wait_recv()
-
-    vec = vec_in[...]
-    for k in range(slots):
-        after = apply(vec, full[k, :n], False) + full[k, n:]
-        out_ref[0, k : k + 1] = jnp.where(live[k], nexts[k] + after[0:1], 0.0)
-
-    @pl.when(place > 0)
-    def _():
-        first_copy.wait_send()
-
-    @pl.when(even)
-    def _():
-        map_copy(acc.at[0], 0, mate).wait_send()
-
-    @pl.when(odd)
-    def _():
-        for r in range(1, rounds):
-            map_copy(acc.at[r], r, partner(r)).wait_send()
-        map_copy(enter, rounds, mate).wait_send()
+            for j in range(half, 0, -1):
+                map_copy(r, me + j, j - 1).wait_send()
 
     @pl.when(passes_on)
     def _():
-        for i in range(2):
-            vec_copy(i).wait_send()
+        for to in range(blocks):
+            vec_copy(to).wait_send()
 
 
 def body(
@@ -382,18 +370,19 @@
         + [
             pltpu.SMEM(counts.shape, jnp.int32),
             pltpu.VMEM((1, n), f32),
-            pltpu.VMEM((rounds + 1, n + PAD, n), f32),
-            pltpu.VMEM((rounds + 1, n + PAD, n), f32),
+            pltpu.VMEM((n + PAD, n), f32),
+            pltpu.VMEM((rounds, n + PAD, n), f32),
             pltpu.VMEM((n + PAD, n), f32),
             pltpu.VMEM((slots, n + PAD, n), f32),
-            pltpu.VMEM((slots, n + PAD, n), f32),
+            pltpu.VMEM((slots, n, 2 * n), jnp.bfloat16),
+            pltpu.VMEM((slots, PAD, n), f32),
             pltpu.VMEM((PAD, n), f32),
             pltpu.VMEM((PAD, n), f32),
             pltpu.SemaphoreType.DMA((len(operands),)),
             pltpu.SemaphoreType.DMA((2,)),
-            pltpu.SemaphoreType.DMA((rounds + 1,)),
-            pltpu.SemaphoreType.DMA((rounds + 1,)),
-            pltpu.SemaphoreType.DMA((2,)),
+            pltpu.SemaphoreType.DMA((blocks,)),
+            pltpu.SemaphoreType.DMA((rounds,)),
+            pltpu.SemaphoreType.DMA((blocks,)),
             pltpu.SemaphoreType.DMA,
         ],
         compiler_params=pltpu.CompilerParams(

time: 23.1 us -> 22.1 us (0.957)
  Pallas kernels: 20.4 us -> 19.4 us
    pallas_call x1, Pallas kernels: 20.4 us -> 19.4 us  [body(): pl.pallas_call(functools.partial(kernel, segs, blocks, rounds), out_shape...]
where the time goes in v3:
time: 22.1 us; the launch traced here: 21.9 us
  Pallas kernels  19.4 us (88%)
  between operations  1.29 us (6%)
  local copies, waits for them, and re-layouts  1.26 us (6%)
    pallas_call x1, Pallas kernels, body(): pl.pallas_call(functools.partial(kernel, segs, blocks, rounds), out_shape...  19.4 us
    squeeze x1, local copies, waits for them, and re-layouts, body(): return (out[0], out[1])  1.26 us

profile of v3, /device:TPU:6, one launch (start us, length us, event | category | flops | bytes accessed | tf_op | source)
XLA Modules:
  0.0 21.9 jit_solution(11814302900665054038)
XLA Ops:
  1.3 19.4 %shard_map.104 = f32[2,4,128]{2,1,0:T(4,128)} custom-call(f32[4,128,128]{2,1,0:T(8,128)} %jac_hbm.1, f32[4,128,128]{2,1,0:T(8,128)} %inv_hbm.1, f32[4,64,128]{2,1,0:T(8,128)} %bitcast.7, f32[4,64]{1,0:T(4,128)} %ctl_hbm.1, f32[4,64]{1,0:T(4,128)} %step_hbm.1, f32[4,128]{1,0:T(4,128)} %traj_hbm.1, f32[1,128]{1,0:T(1,128)} %bitcast.8, f32[1,128]{1,0:T(1,128)} %bitcast.9, ...), custom_call_target="tpu_custom_call" | custom-call | tf_op jit(solution)/shard_map/pallas_call | solution.py:364
  20.6 1.3 %slice_bitcast_fusion = (f32[4,128]{1,0:T(4,128)}, f32[4,128]{1,0:T(4,128)}) fusion(f32[2,4,128]{2,1,0:T(4,128)} %shard_map.104), kind=kLoop, calls=%fused_computation | loop fusion | bytes 8192 | tf_op jit(solution)/shard_map/squeeze | solution.py:392

commit v4 on v3

--- a/solution.py
+++ b/solution.py
@@ -234,6 +234,21 @@
 
     acc[n:] = fold_vec(0, slots)
 
+    def at_front(r):
+        return jnp.logical_and(seg == 0, me < (2 << r))
+
+    def gives(r):
+        half = 1 << r
+        return jnp.logical_and(me % (2 * half) == half - 1, jnp.logical_not(at_front(r)))
+
+    def gathers(r):
+        half = 1 << r
+        inner = jnp.logical_and(me % (2 * half) == 2 * half - 1, me < blocks - 1)
+        return jnp.logical_and(inner, jnp.logical_not(at_front(r)))
+
+    def takes(r):
+        return jnp.logical_and((me // (1 << r)) % 2 == 1, jnp.logical_not(at_front(r)))
+
     def map_copy(r, to, j):
         return pltpu.make_async_remote_copy(
             src_ref=acc,
@@ -245,14 +260,13 @@
         )
 
     for r in range(rounds):
-        half = 1 << r
-
-        @pl.when(me % (2 * half) == half - 1)
-        def _():
-            for j in range(half, 0, -1):
+
+        @pl.when(gives(r))
+        def _():
+            for j in range(1 << r, 0, -1):
                 map_copy(r, me + j, j - 1).start()
 
-        @pl.when(jnp.logical_and(me % (2 * half) == 2 * half - 1, me < blocks - 1))
+        @pl.when(gathers(r))
         def _():
             map_copy(r, me, 0).wait_recv()
             acc[...] = compose(got[r], acc[...])
@@ -261,43 +275,54 @@
         maps[k, :n] = fold(0, k + 1)
         maps[k, n:] = fold_vec(0, k + 1)
 
-    enter[:n] = eye
-    enter[n:] = jnp.zeros((PAD, n), jnp.float32)
-    for r in reversed(range(rounds)):
-        half = 1 << r
-        done = jnp.logical_and(me % (2 * half) == 2 * half - 1, me < blocks - 1)
-
-        @pl.when((me // half) % 2 == 1)
-        def _():
-            @pl.when(jnp.logical_not(done))
-            def _():
-                map_copy(r, me, 0).wait_recv()
-
-            enter[...] = compose(enter[...], got[r])
-
-    start = enter[...]
-    for k in reversed(range(slots)):
-        rows = compose(start, maps[k])
+    some = takes(0)
+    for r in range(1, rounds):
+        some = jnp.logical_or(some, takes(r))
+
+    def keep(k, rows):
         full[k] = jnp.concatenate(halves(rows[:n]), axis=1).astype(jnp.bfloat16)
         tails[k] = rows[n:]
 
-    def vec_copy(to):
+    @pl.when(jnp.logical_not(some))
+    def _():
+        for k in range(slots):
+            keep(k, maps[k])
+
+    @pl.when(some)
+    def _():
+        enter[:n] = eye
+        enter[n:] = jnp.zeros((PAD, n), jnp.float32)
+        for r in reversed(range(rounds)):
+
+            @pl.when(takes(r))
+            def _():
+                @pl.when(jnp.logical_not(gathers(r)))
+                def _():
+                    map_copy(r, me, 0).wait_recv()
+
+                enter[...] = compose(enter[...], got[r])
+
+        start = enter[...]
+        for k in reversed(range(slots)):
+            keep(k, compose(start, maps[k]))
+
+    def vec_copy(group, to):
         return pltpu.make_async_remote_copy(
             src_ref=vec_out,
             dst_ref=vec_in,
             send_sem=vec_send.at[to],
             recv_sem=vec_recv,
-            device_id=(jnp.minimum(seg + 1, segs - 1), to),
+            device_id=(group, to),
             device_id_type=MESH,
         )
 
-    @pl.when(seg == 0)
+    @pl.when(place == 0)
     def _():
         vec_in[...] = eight(gap[...])
 
-    @pl.when(seg > 0)
-    def _():
-        vec_copy(0).wait_recv()
+    @pl.when(place > 0)
+    def _():
+        vec_copy(seg, 0).wait_recv()
 
     stacked = jnp.concatenate(halves(vec_in[...]), axis=0).astype(jnp.bfloat16)
 
@@ -310,7 +335,15 @@
     def _():
         vec_out[...] = after(slots - 1)
         for to in range(blocks - 1, -1, -1):
-            vec_copy(to).start()
+            vec_copy(seg + 1, to).start()
+
+    for r in range(rounds):
+
+        @pl.when(place == (1 << r) - 1)
+        def _():
+            vec_out[...] = after(slots - 1)
+            for j in range(1 << r, 0, -1):
+                vec_copy(seg, me + j).start()
 
     for k in range(slots):
         out_ref[0, k : k + 1] = jnp.where(live[k], nexts[k] + after(k)[0:1], 0.0)
@@ -320,17 +353,21 @@
         first_copy.wait_send()
 
     for r in range(rounds):
-        half = 1 << r
-
-        @pl.when(me % (2 * half) == half - 1)
-        def _():
-            for j in range(half, 0, -1):
+
+        @pl.when(gives(r))
+        def _():
+            for j in range(1 << r, 0, -1):
                 map_copy(r, me + j, j - 1).wait_send()
 
+        @pl.when(place == (1 << r) - 1)
+        def _():
+            for j in range(1 << r, 0, -1):
+                vec_copy(seg, me + j).wait_send()
+
     @pl.when(passes_on)
     def _():
         for to in range(blocks):
-            vec_copy(to).wait_send()
+            vec_copy(seg + 1, to).wait_send()
 
 
 def body(

time: 22.1 us -> 21.5 us (0.973)
  Pallas kernels: 19.4 us -> 18.7 us
    pallas_call x1, Pallas kernels: 19.4 us -> 18.7 us  [body(): pl.pallas_call(functools.partial(kernel, segs, blocks, rounds), out_shape...]
where the time goes in v4:
time: 21.5 us; the launch traced here: 21.3 us
  Pallas kernels  18.7 us (87%)
  between operations  1.29 us (6%)
  local copies, waits for them, and re-layouts  1.26 us (6%)
    pallas_call x1, Pallas kernels, body(): pl.pallas_call(functools.partial(kernel, segs, blocks, rounds), out_shape...  18.7 us
    squeeze x1, local copies, waits for them, and re-layouts, body(): return (out[0], out[1])  1.26 us

profile of v4, /device:TPU:6, one launch (start us, length us, event | category | flops | bytes accessed | tf_op | source)
XLA Modules:
  0.0 21.3 jit_solution(6415342960623434091)
XLA Ops:
  1.3 18.7 %shard_map.104 = f32[2,4,128]{2,1,0:T(4,128)} custom-call(f32[4,128,128]{2,1,0:T(8,128)} %jac_hbm.1, f32[4,128,128]{2,1,0:T(8,128)} %inv_hbm.1, f32[4,64,128]{2,1,0:T(8,128)} %bitcast.7, f32[4,64]{1,0:T(4,128)} %ctl_hbm.1, f32[4,64]{1,0:T(4,128)} %step_hbm.1, f32[4,128]{1,0:T(4,128)} %traj_hbm.1, f32[1,128]{1,0:T(1,128)} %bitcast.8, f32[1,128]{1,0:T(1,128)} %bitcast.9, ...), custom_call_target="tpu_custom_call" | custom-call | tf_op jit(solution)/shard_map/pallas_call | solution.py:401
  20.0 1.3 %slice_bitcast_fusion = (f32[4,128]{1,0:T(4,128)}, f32[4,128]{1,0:T(4,128)}) fusion(f32[2,4,128]{2,1,0:T(4,128)} %shard_map.104), kind=kLoop, calls=%fused_computation | loop fusion | bytes 8192 | tf_op jit(solution)/shard_map/squeeze | solution.py:429

commit v5 on v4

--- a/solution.py
+++ b/solution.py
@@ -15,10 +15,16 @@
     return high, x - high
 
 
+def parts(x):
+    if isinstance(x, tuple):
+        return x
+    return tuple(h.astype(jnp.bfloat16) for h in halves(x))
+
+
 def product(left, right, turned):
     dims = (((1,), (1 if turned else 0,)), ((), ()))
-    lh, ll = (h.astype(jnp.bfloat16) for h in halves(left))
-    rh, rl = (h.astype(jnp.bfloat16) for h in halves(right))
+    lh, ll = parts(left)
+    rh, rl = parts(right)
     rows = jnp.concatenate([lh, ll], axis=1)
     if turned:
         other = jnp.concatenate([rh, rl], axis=0)
@@ -35,7 +41,7 @@
     count = rows.shape[0]
     dims = (((1,), (1 if turned else 0,)), ((), ()))
     stacked = jnp.concatenate(halves(rows), axis=0).astype(jnp.bfloat16)
-    rh, rl = (h.astype(jnp.bfloat16) for h in halves(right))
+    rh, rl = parts(right)
     other = jnp.concatenate([rh, rl], axis=0 if turned else 1)
     out = lax.dot_general(stacked, other, dims, preferred_element_type=jnp.float32)
     width = out.shape[1] // 2
@@ -113,9 +119,6 @@
             )
         )
     ]
-    for load in loads:
-        load.start()
-
     barrier = pltpu.get_barrier_semaphore()
 
     def tell(s, b):
@@ -140,6 +143,8 @@
         tell(seg - 1, blocks - 1)
 
     peers += jnp.where(passes_on, blocks, 0)
+    for load in loads:
+        load.start()
     pl.semaphore_wait(barrier, peers)
 
     ahead = jnp.maximum(place - 1, 0)
@@ -164,17 +169,12 @@
         load.wait()
     live = [k < count[0] for k in range(slots)]
 
-    @pl.when(place < last)
-    def _():
-        first_copy.wait_recv()
-
-    @pl.when(place == last)
-    def _():
-        first[...] = term[...]
-
+    jacs = [parts(jac[k]) for k in range(slots)]
+    invs = [parts(inv[k]) for k in range(slots)]
     trans = [
-        eye + jnp.where(live[k], product(inv[k], jac[k], False), 0.0) for k in range(slots)
+        eye + jnp.where(live[k], product(invs[k], jacs[k], False), 0.0) for k in range(slots)
     ]
+    steps = [parts(t) for t in trans]
     known = {}
 
     def fold(lo, hi):
@@ -185,12 +185,29 @@
                 mid = (lo + hi) // 2 if lo or hi == slots else hi - 1
                 early = fold(lo, mid)
                 if hi - mid == 1:
-                    known[lo, hi] = product(early, trans[mid], True)
+                    known[lo, hi] = product(early, steps[mid], True)
                 else:
                     known[lo, hi] = product(early, fold(mid, hi), False)
         return known[lo, hi]
 
     acc[:n] = fold(0, slots)
+    for k in range(slots):
+        maps[k, :n] = fold(0, k + 1)
+    forced = []
+    for k in range(slots):
+        both = jnp.concatenate(
+            [ctl[k : k + 1], step[k : k + 1], jnp.zeros((PAD - 2, ctl.shape[1]), jnp.float32)],
+            axis=0,
+        )
+        forced.append(apply(both, inp[k], False))
+
+    @pl.when(place < last)
+    def _():
+        first_copy.wait_recv()
+
+    @pl.when(place == last)
+    def _():
+        first[...] = term[...]
 
     upcoming = first[...]
 
@@ -206,15 +223,11 @@
             nxt = upcoming
         nexts.append(nxt)
         change = eight(nxt - now)
-        both = jnp.concatenate(
-            [ctl[k : k + 1], step[k : k + 1], jnp.zeros((PAD - 2, ctl.shape[1]), jnp.float32)],
-            axis=0,
-        )
-        moved = apply(both, inp[k], False)
-        mid = apply(change, jac[k], True) * (1.0 / 12.0) - eight(0.5 * (nxt + now))
-        defect = change + apply(mid, jac[k], True) - eight(moved[0:1])
+        moved = forced[k]
+        mid = apply(change, jacs[k], True) * (1.0 / 12.0) - eight(0.5 * (nxt + now))
+        defect = change + apply(mid, jacs[k], True) - eight(moved[0:1])
         out_ref[1, k : k + 1] = jnp.where(live[k], defect[0:1], 0.0)
-        offset = apply(eight(moved[1:2]) - defect, inv[k], True)
+        offset = apply(eight(moved[1:2]) - defect, invs[k], True)
         offsets.append(jnp.where(live[k], offset, 0.0))
     known_vec = {}
 
@@ -226,7 +239,7 @@
                 mid = (lo + hi) // 2 if lo or hi == slots else hi - 1
                 early = fold_vec(lo, mid)
                 if hi - mid == 1:
-                    moved = apply(early, trans[mid], True)
+                    moved = apply(early, steps[mid], True)
                 else:
                     moved = apply(early, fold(mid, hi), False)
                 known_vec[lo, hi] = moved + fold_vec(mid, hi)
@@ -272,7 +285,6 @@
             acc[...] = compose(got[r], acc[...])
 
     for k in range(slots):
-        maps[k, :n] = fold(0, k + 1)
         maps[k, n:] = fold_vec(0, k + 1)
 
     some = takes(0)

time: 21.5 us -> 21.6 us (level)
  no operation moved by 1% of the time
where the time goes in v5:
time: 21.6 us; the launch traced here: 21.4 us
  Pallas kernels  18.8 us (87%)
  between operations  1.29 us (6%)
  local copies, waits for them, and re-layouts  1.26 us (6%)
    pallas_call x1, Pallas kernels, body(): pl.pallas_call(functools.partial(kernel, segs, blocks, rounds), out_shape...  18.8 us
    squeeze x1, local copies, waits for them, and re-layouts, body(): return (out[0], out[1])  1.26 us

profile of v5, /device:TPU:6, one launch (start us, length us, event | category | flops | bytes accessed | tf_op | source)
XLA Modules:
  0.0 21.4 jit_solution(4804418716276745843)
XLA Ops:
  1.3 18.8 %shard_map.104 = f32[2,4,128]{2,1,0:T(4,128)} custom-call(f32[4,128,128]{2,1,0:T(8,128)} %jac_hbm.1, f32[4,128,128]{2,1,0:T(8,128)} %inv_hbm.1, f32[4,64,128]{2,1,0:T(8,128)} %bitcast.7, f32[4,64]{1,0:T(4,128)} %ctl_hbm.1, f32[4,64]{1,0:T(4,128)} %step_hbm.1, f32[4,128]{1,0:T(4,128)} %traj_hbm.1, f32[1,128]{1,0:T(1,128)} %bitcast.8, f32[1,128]{1,0:T(1,128)} %bitcast.9, ...), custom_call_target="tpu_custom_call" | custom-call | tf_op jit(solution)/shard_map/pallas_call | solution.py:413
  20.1 1.3 %slice_bitcast_fusion = (f32[4,128]{1,0:T(4,128)}, f32[4,128]{1,0:T(4,128)}) fusion(f32[2,4,128]{2,1,0:T(4,128)} %shard_map.104), kind=kLoop, calls=%fused_computation | loop fusion | bytes 8192 | tf_op jit(solution)/shard_map/squeeze | solution.py:441

commit v6 on v5

--- a/solution.py
+++ b/solution.py
@@ -304,7 +304,7 @@
     def _():
         enter[:n] = eye
         enter[n:] = jnp.zeros((PAD, n), jnp.float32)
-        for r in reversed(range(rounds)):
+        for r in range(rounds):
 
             @pl.when(takes(r))
             def _():
@@ -312,7 +312,7 @@
                 def _():
                     map_copy(r, me, 0).wait_recv()
 
-                enter[...] = compose(enter[...], got[r])
+                enter[...] = compose(got[r], enter[...])
 
         start = enter[...]
         for k in reversed(range(slots)):

time: 21.6 us -> 21.2 us (0.981)
  Pallas kernels: 18.8 us -> 18.5 us
    pallas_call x1, Pallas kernels: 18.8 us -> 18.5 us  [body(): pl.pallas_call(functools.partial(kernel, segs, blocks, rounds), out_shape...]
where the time goes in v6:
time: 21.2 us; the launch traced here: 21 us
  Pallas kernels  18.5 us (87%)
  between operations  1.29 us (6%)
  local copies, waits for them, and re-layouts  1.26 us (6%)
    pallas_call x1, Pallas kernels, body(): pl.pallas_call(functools.partial(kernel, segs, blocks, rounds), out_shape...  18.5 us
    squeeze x1, local copies, waits for them, and re-layouts, body(): return (out[0], out[1])  1.26 us

profile of v6, /device:TPU:6, one launch (start us, length us, event | category | flops | bytes accessed | tf_op | source)
XLA Modules:
  0.0 21.0 jit_solution(15975266993079304643)
XLA Ops:
  1.3 18.5 %shard_map.104 = f32[2,4,128]{2,1,0:T(4,128)} custom-call(f32[4,128,128]{2,1,0:T(8,128)} %jac_hbm.1, f32[4,128,128]{2,1,0:T(8,128)} %inv_hbm.1, f32[4,64,128]{2,1,0:T(8,128)} %bitcast.7, f32[4,64]{1,0:T(4,128)} %ctl_hbm.1, f32[4,64]{1,0:T(4,128)} %step_hbm.1, f32[4,128]{1,0:T(4,128)} %traj_hbm.1, f32[1,128]{1,0:T(1,128)} %bitcast.8, f32[1,128]{1,0:T(1,128)} %bitcast.9, ...), custom_call_target="tpu_custom_call" | custom-call | tf_op jit(solution)/shard_map/pallas_call | solution.py:413
  19.7 1.3 %slice_bitcast_fusion = (f32[4,128]{1,0:T(4,128)}, f32[4,128]{1,0:T(4,128)}) fusion(f32[2,4,128]{2,1,0:T(4,128)} %shard_map.104), kind=kLoop, calls=%fused_computation | loop fusion | bytes 8192 | tf_op jit(solution)/shard_map/squeeze | solution.py:441
